TPU v7x, 32 devices: a whole 2x2x4 slice. The times are simulated.
32 devices in a mesh: layer: 8 (over y, x, core), row: 4 (over z).
Axes of the slice: x: 2, y: 2, z: 4, core: 2. Of those that a mesh axis runs over, the one named last changes fastest.
Arguments:
- operator: bfloat16 [2, 8, 4096, 4096], P(None, 'layer', 'row'), may hold values from -0.0625 to 0.0625
- sources: bfloat16 [2, 8, 4096, 512], P(None, 'layer', 'row'), may hold values from -3 to 3
- boundary: bfloat16 [2, 4096, 512], P(None, 'row'), may hold values from -6 to 6
Outputs:
- traces: float32 [2, 8, 4096, 512], P(None, 'layer', 'row')
All inputs are finite; a program needn't handle non-finite values.
Results may differ from a plain program's by a relative error of at most 0.015.
Values may be sent and summed in bfloat16 or wider, within the bound.
A program may use at most 128 MiB of HBM per device.

v0:
```python
import jax
import jax.numpy as jnp
from jax import lax
from jax.sharding import PartitionSpec as P

B = 128


def shifted(value, axis, by):
    devices = lax.axis_size(axis)
    pairs = [(i, i + by) for i in range(devices) if 0 <= i + by < devices]
    return lax.ppermute(value, axis, pairs)


def right_product(left, weights):
    return lax.dot_general(
        left, weights, (((1,), (1,)), ((), ())), preferred_element_type=jnp.float32
    )


def on_device(operator, sources, boundary):
    real = operator[0, 0]
    imag = operator[1, 0]
    local_rows = real.shape[0]
    total = sources.shape[3]
    own_sources = jnp.swapaxes(sources[:, 0], 1, 2)
    entering_all = jnp.swapaxes(boundary, 1, 2)
    width = B // 2
    count = total // width
    depth = lax.axis_size("layer")
    level = lax.axis_index("layer")
    beats = count + depth - 1
    first_received = jnp.zeros((2, width, local_rows), jnp.bfloat16)

    def beat(step, carry):
        received, collected = carry
        batch = step - level
        active = jnp.logical_and(batch >= 0, batch < count)
        column = jnp.clip(batch, 0, count - 1) * width
        entering = lax.dynamic_slice_in_dim(entering_all, column, width, 1)
        incoming = jnp.where(level == 0, entering, received)
        gathered = lax.all_gather(incoming, "row", axis=2, tiled=True)

        def compute():
            trace_re = gathered[0]
            trace_im = gathered[1]
            part_re = right_product(trace_re, real) - right_product(trace_im, imag)
            part_im = right_product(trace_im, real) + right_product(trace_re, imag)
            product = jnp.stack([part_re, part_im], axis=0)
            return product + lax.dynamic_slice_in_dim(own_sources, column, width, 1).astype(
                jnp.float32
            )

        def skipped():
            return jnp.zeros((2, width, local_rows), jnp.float32)

        fresh = lax.cond(active, compute, skipped)
        updated = lax.dynamic_update_slice(collected, fresh, (jnp.int32(0), column, jnp.int32(0)))
        collected = jnp.where(active, updated, collected)
        outgoing = fresh.astype(jnp.bfloat16)
        received = shifted(outgoing, "layer", 1)
        return (received, collected)

    start = (first_received, jnp.zeros((2, total, local_rows), jnp.float32))
    received, collected = lax.fori_loop(0, beats, beat, start)
    return jnp.swapaxes(collected, 1, 2)[:, None]


def solution(mesh):
    placed = (P(None, "layer", "row", None), P(None, "layer", "row", None), P(None, "row", None))
    return jax.shard_map(
        on_device,
        mesh=mesh,
        in_specs=placed,
        out_specs=P(None, "layer", "row", None),
        check_vma=False,
    )
```

profile of v0, /device:TPU:7, one launch (start us, length us, event | category | flops | bytes accessed | tf_op | source)
XLA Modules:
  0.0 850.6 jit_solution(7751190147368312182)
XLA Ops:
  13.5 11.7 %slice_bitcast_fusion = (bf16[1024,4096]{1,0:T(8,128)(2,1)}, bf16[1024,4096]{1,0:T(8,128)(2,1)}) fusion(bf16[2,1,1024,4096]{3,2,1,0:T(8,128)(2,1)} %param.7), kind=kLoop, calls=%fused_computation.17 | loop fusion | bytes 33554432 | tf_op jit(solution)/shard_map/squeeze | solution.py:23
  27.6 811.1 %while.16 = (s32[]{:T(128)}, bf16[2,64,1024]{2,1,0:T(8,128)(2,1)S(1)}, f32[2,512,1024]{2,1,0:T(8,128)}, s32[]{:T(128)}, pred[]{:T(512)}, /*index=5*/bf16[2,512,1...) while((s32[]{:T(128)}, ...), condition=%wide.region_3.4_spmd, body=%wide.region_0.3_spmd.sunk | while | flops 2148401152 | bytes 109052440 | solution.py:65
  29.4 29.6 %all-gather.2.cloned.1.call-done = bf16[2,64,4096]{2,1,0:T(8,128)(2,1)} async-done(((bf16[2,64,1024]{2,1,0:T(8,128)(2,1)}), bf16[2,64,4096]{2,1,0:T(8,128)(2,1)}) %all-gather.2.cloned.1.call-update) | async-done | bytes 1048592 | tf_op jit(solution)/shard_map/while/body/eval_jaxpr/all_gather | solution.py:42
  66.5 40.6 %all-gather.2.cloned.1.call-done = bf16[2,64,4096]{2,1,0:T(8,128)(2,1)} async-done(((bf16[2,64,1024]{2,1,0:T(8,128)(2,1)}), bf16[2,64,4096]{2,1,0:T(8,128)(2,1)}) %all-gather.2.cloned.1.call-update) | async-done | bytes 1048592 | tf_op jit(solution)/shard_map/while/body/eval_jaxpr/all_gather | solution.py:42
  114.7 45.0 %all-gather.2.cloned.1.call-done = bf16[2,64,4096]{2,1,0:T(8,128)(2,1)} async-done(((bf16[2,64,1024]{2,1,0:T(8,128)(2,1)}), bf16[2,64,4096]{2,1,0:T(8,128)(2,1)}) %all-gather.2.cloned.1.call-update) | async-done | bytes 1048592 | tf_op jit(solution)/shard_map/while/body/eval_jaxpr/all_gather | solution.py:42
  167.2 46.4 %all-gather.2.cloned.1.call-done = bf16[2,64,4096]{2,1,0:T(8,128)(2,1)} async-done(((bf16[2,64,1024]{2,1,0:T(8,128)(2,1)}), bf16[2,64,4096]{2,1,0:T(8,128)(2,1)}) %all-gather.2.cloned.1.call-update) | async-done | bytes 1048592 | tf_op jit(solution)/shard_map/while/body/eval_jaxpr/all_gather | solution.py:42
  221.1 46.4 %all-gather.2.cloned.1.call-done = bf16[2,64,4096]{2,1,0:T(8,128)(2,1)} async-done(((bf16[2,64,1024]{2,1,0:T(8,128)(2,1)}), bf16[2,64,4096]{2,1,0:T(8,128)(2,1)}) %all-gather.2.cloned.1.call-update) | async-done | bytes 1048592 | tf_op jit(solution)/shard_map/while/body/eval_jaxpr/all_gather | solution.py:42
  275.1 47.3 %all-gather.2.cloned.1.call-done = bf16[2,64,4096]{2,1,0:T(8,128)(2,1)} async-done(((bf16[2,64,1024]{2,1,0:T(8,128)(2,1)}), bf16[2,64,4096]{2,1,0:T(8,128)(2,1)}) %all-gather.2.cloned.1.call-update) | async-done | bytes 1048592 | tf_op jit(solution)/shard_map/while/body/eval_jaxpr/all_gather | solution.py:42
  329.9 47.7 %all-gather.2.cloned.1.call-done = bf16[2,64,4096]{2,1,0:T(8,128)(2,1)} async-done(((bf16[2,64,1024]{2,1,0:T(8,128)(2,1)}), bf16[2,64,4096]{2,1,0:T(8,128)(2,1)}) %all-gather.2.cloned.1.call-update) | async-done | bytes 1048592 | tf_op jit(solution)/shard_map/while/body/eval_jaxpr/all_gather | solution.py:42
  380.9 18.1 %collective-permute-done = bf16[2,64,1024]{2,1,0:T(8,128)(2,1)S(1)} collective-permute-done((bf16[2,64,1024]{2,1,0:T(8,128)(2,1)S(1)}, bf16[2,64,1024]{2,1,0:T(8,128)(2,1)S(1)}, u32[]{:S(2)}, u32[]{:S(2)}) %collective-permute-start) | collective-permute-done | bytes 262176 | tf_op jit(solution)/shard_map/while/body/eval_jaxpr/ppermute | solution.py:12
  400.7 32.0 %all-gather.2.cloned.1.call-done = bf16[2,64,4096]{2,1,0:T(8,128)(2,1)} async-done(((bf16[2,64,1024]{2,1,0:T(8,128)(2,1)}), bf16[2,64,4096]{2,1,0:T(8,128)(2,1)}) %all-gather.2.cloned.1.call-update) | async-done | bytes 1048592 | tf_op jit(solution)/shard_map/while/body/eval_jaxpr/all_gather | solution.py:42
  432.7 15.7 %conditional.2 = (f32[2,64,1024]{2,1,0:T(8,128)S(1)}) conditional(s32[]{:T(128)} %convert_element_type.24, () %tuple.44, (bf16[2,64,4096]{2,1,0:T(8,128)(2,1)}, bf16[1024,4096]{1,0:T(8,128)(2,1)}, bf16[1024,4096]{1,0:T(8,128)(2,1)}, s32[]{:T(128)}, bf16[2,512,1024]{2,1,0:T(8,128)(2,1)S(1)}) %tuple.45), branch_computations={%region_1.1_spmd, %region_2.2_spmd} | conditional | flops 2148007936 | bytes 101449880 | solution.py:57
  455.9 32.0 %all-gather.2.cloned.1.call-done = bf16[2,64,4096]{2,1,0:T(8,128)(2,1)} async-done(((bf16[2,64,1024]{2,1,0:T(8,128)(2,1)}), bf16[2,64,4096]{2,1,0:T(8,128)(2,1)}) %all-gather.2.cloned.1.call-update) | async-done | bytes 1048592 | tf_op jit(solution)/shard_map/while/body/eval_jaxpr/all_gather | solution.py:42
  487.9 15.7 %conditional.2 = (f32[2,64,1024]{2,1,0:T(8,128)S(1)}) conditional(s32[]{:T(128)} %convert_element_type.24, () %tuple.44, (bf16[2,64,4096]{2,1,0:T(8,128)(2,1)}, bf16[1024,4096]{1,0:T(8,128)(2,1)}, bf16[1024,4096]{1,0:T(8,128)(2,1)}, s32[]{:T(128)}, bf16[2,512,1024]{2,1,0:T(8,128)(2,1)S(1)}) %tuple.45), branch_computations={%region_1.1_spmd, %region_2.2_spmd} | conditional | flops 2148007936 | bytes 101449880 | solution.py:57
  487.9 6.3 fusion.2
  511.1 31.7 %all-gather.2.cloned.1.call-done = bf16[2,64,4096]{2,1,0:T(8,128)(2,1)} async-done(((bf16[2,64,1024]{2,1,0:T(8,128)(2,1)}), bf16[2,64,4096]{2,1,0:T(8,128)(2,1)}) %all-gather.2.cloned.1.call-update) | async-done | bytes 1048592 | tf_op jit(solution)/shard_map/while/body/eval_jaxpr/all_gather | solution.py:42
  542.8 15.7 %conditional.2 = (f32[2,64,1024]{2,1,0:T(8,128)S(1)}) conditional(s32[]{:T(128)} %convert_element_type.24, () %tuple.44, (bf16[2,64,4096]{2,1,0:T(8,128)(2,1)}, bf16[1024,4096]{1,0:T(8,128)(2,1)}, bf16[1024,4096]{1,0:T(8,128)(2,1)}, s32[]{:T(128)}, bf16[2,512,1024]{2,1,0:T(8,128)(2,1)S(1)}) %tuple.45), branch_computations={%region_1.1_spmd, %region_2.2_spmd} | conditional | flops 2148007936 | bytes 101449880 | solution.py:57
  565.9 32.0 %all-gather.2.cloned.1.call-done = bf16[2,64,4096]{2,1,0:T(8,128)(2,1)} async-done(((bf16[2,64,1024]{2,1,0:T(8,128)(2,1)}), bf16[2,64,4096]{2,1,0:T(8,128)(2,1)}) %all-gather.2.cloned.1.call-update) | async-done | bytes 1048592 | tf_op jit(solution)/shard_map/while/body/eval_jaxpr/all_gather | solution.py:42
  598.0 15.7 %conditional.2 = (f32[2,64,1024]{2,1,0:T(8,128)S(1)}) conditional(s32[]{:T(128)} %convert_element_type.24, () %tuple.44, (bf16[2,64,4096]{2,1,0:T(8,128)(2,1)}, bf16[1024,4096]{1,0:T(8,128)(2,1)}, bf16[1024,4096]{1,0:T(8,128)(2,1)}, s32[]{:T(128)}, bf16[2,512,1024]{2,1,0:T(8,128)(2,1)S(1)}) %tuple.45), branch_computations={%region_1.1_spmd, %region_2.2_spmd} | conditional | flops 2148007936 | bytes 101449880 | solution.py:57
  598.0 6.3 fusion.2
  621.1 31.7 %all-gather.2.cloned.1.call-done = bf16[2,64,4096]{2,1,0:T(8,128)(2,1)} async-done(((bf16[2,64,1024]{2,1,0:T(8,128)(2,1)}), bf16[2,64,4096]{2,1,0:T(8,128)(2,1)}) %all-gather.2.cloned.1.call-update) | async-done | bytes 1048592 | tf_op jit(solution)/shard_map/while/body/eval_jaxpr/all_gather | solution.py:42
  652.8 15.7 %conditional.2 = (f32[2,64,1024]{2,1,0:T(8,128)S(1)}) conditional(s32[]{:T(128)} %convert_element_type.24, () %tuple.44, (bf16[2,64,4096]{2,1,0:T(8,128)(2,1)}, bf16[1024,4096]{1,0:T(8,128)(2,1)}, bf16[1024,4096]{1,0:T(8,128)(2,1)}, s32[]{:T(128)}, bf16[2,512,1024]{2,1,0:T(8,128)(2,1)S(1)}) %tuple.45), branch_computations={%region_1.1_spmd, %region_2.2_spmd} | conditional | flops 2148007936 | bytes 101449880 | solution.py:57
  652.8 6.3 fusion.2
  676.0 32.0 %all-gather.2.cloned.1.call-done = bf16[2,64,4096]{2,1,0:T(8,128)(2,1)} async-done(((bf16[2,64,1024]{2,1,0:T(8,128)(2,1)}), bf16[2,64,4096]{2,1,0:T(8,128)(2,1)}) %all-gather.2.cloned.1.call-update) | async-done | bytes 1048592 | tf_op jit(solution)/shard_map/while/body/eval_jaxpr/all_gather | solution.py:42
  708.0 15.7 %conditional.2 = (f32[2,64,1024]{2,1,0:T(8,128)S(1)}) conditional(s32[]{:T(128)} %convert_element_type.24, () %tuple.44, (bf16[2,64,4096]{2,1,0:T(8,128)(2,1)}, bf16[1024,4096]{1,0:T(8,128)(2,1)}, bf16[1024,4096]{1,0:T(8,128)(2,1)}, s32[]{:T(128)}, bf16[2,512,1024]{2,1,0:T(8,128)(2,1)S(1)}) %tuple.45), branch_computations={%region_1.1_spmd, %region_2.2_spmd} | conditional | flops 2148007936 | bytes 101449880 | solution.py:57
  708.0 6.3 fusion.2
  731.2 31.7 %all-gather.2.cloned.1.call-done = bf16[2,64,4096]{2,1,0:T(8,128)(2,1)} async-done(((bf16[2,64,1024]{2,1,0:T(8,128)(2,1)}), bf16[2,64,4096]{2,1,0:T(8,128)(2,1)}) %all-gather.2.cloned.1.call-update) | async-done | bytes 1048592 | tf_op jit(solution)/shard_map/while/body/eval_jaxpr/all_gather | solution.py:42
  762.9 15.7 %conditional.2 = (f32[2,64,1024]{2,1,0:T(8,128)S(1)}) conditional(s32[]{:T(128)} %convert_element_type.24, () %tuple.44, (bf16[2,64,4096]{2,1,0:T(8,128)(2,1)}, bf16[1024,4096]{1,0:T(8,128)(2,1)}, bf16[1024,4096]{1,0:T(8,128)(2,1)}, s32[]{:T(128)}, bf16[2,512,1024]{2,1,0:T(8,128)(2,1)S(1)}) %tuple.45), branch_computations={%region_1.1_spmd, %region_2.2_spmd} | conditional | flops 2148007936 | bytes 101449880 | solution.py:57
  762.9 6.3 fusion.2
  786.0 31.7 %all-gather.2.cloned.1.call-done = bf16[2,64,4096]{2,1,0:T(8,128)(2,1)} async-done(((bf16[2,64,1024]{2,1,0:T(8,128)(2,1)}), bf16[2,64,4096]{2,1,0:T(8,128)(2,1)}) %all-gather.2.cloned.1.call-update) | async-done | bytes 1048592 | tf_op jit(solution)/shard_map/while/body/eval_jaxpr/all_gather | solution.py:42
  817.7 15.7 %conditional.2 = (f32[2,64,1024]{2,1,0:T(8,128)S(1)}) conditional(s32[]{:T(128)} %convert_element_type.24, () %tuple.44, (bf16[2,64,4096]{2,1,0:T(8,128)(2,1)}, bf16[1024,4096]{1,0:T(8,128)(2,1)}, bf16[1024,4096]{1,0:T(8,128)(2,1)}, s32[]{:T(128)}, bf16[2,512,1024]{2,1,0:T(8,128)(2,1)S(1)}) %tuple.45), branch_computations={%region_1.1_spmd, %region_2.2_spmd} | conditional | flops 2148007936 | bytes 101449880 | solution.py:57
  817.7 6.3 fusion.2
  (214 shorter events, 210.9 us)
Async XLA Ops:
  27.6 31.4 %all-gather.2.cloned.1.call-start = ((), (), s32[]{:S(2)}) async-start(), calls=%async_computation | async-start | bytes 1310720 | tf_op jit(solution)/shard_map/while/body/eval_jaxpr/all_gather | solution.py:42
  61.0 3.7 collective-permute-start
  64.7 42.4 %all-gather.2.cloned.1.call-start = ((), (), s32[]{:S(2)}) async-start(), calls=%async_computation | async-start | bytes 1310720 | tf_op jit(solution)/shard_map/while/body/eval_jaxpr/all_gather | solution.py:42
  109.1 3.7 collective-permute-start
  112.9 46.8 %all-gather.2.cloned.1.call-start = ((), (), s32[]{:S(2)}) async-start(), calls=%async_computation | async-start | bytes 1310720 | tf_op jit(solution)/shard_map/while/body/eval_jaxpr/all_gather | solution.py:42
  161.7 3.7 collective-permute-start
  165.4 48.2 %all-gather.2.cloned.1.call-start = ((), (), s32[]{:S(2)}) async-start(), calls=%async_computation | async-start | bytes 1310720 | tf_op jit(solution)/shard_map/while/body/eval_jaxpr/all_gather | solution.py:42
  215.6 3.7 collective-permute-start
  219.3 48.2 %all-gather.2.cloned.1.call-start = ((), (), s32[]{:S(2)}) async-start(), calls=%async_computation | async-start | bytes 1310720 | tf_op jit(solution)/shard_map/while/body/eval_jaxpr/all_gather | solution.py:42
  269.6 3.7 collective-permute-start
  273.3 49.1 %all-gather.2.cloned.1.call-start = ((), (), s32[]{:S(2)}) async-start(), calls=%async_computation | async-start | bytes 1310720 | tf_op jit(solution)/shard_map/while/body/eval_jaxpr/all_gather | solution.py:42
  324.4 3.7 collective-permute-start
  328.1 49.4 %all-gather.2.cloned.1.call-start = ((), (), s32[]{:S(2)}) async-start(), calls=%async_computation | async-start | bytes 1310720 | tf_op jit(solution)/shard_map/while/body/eval_jaxpr/all_gather | solution.py:42
  379.6 19.4 %collective-permute-start = (bf16[2,64,1024]{2,1,0:T(8,128)(2,1)S(1)}, bf16[2,64,1024]{2,1,0:T(8,128)(2,1)S(1)}, u32[]{:S(2)}, u32[]{:S(2)}) collective-permute-start(bf16[2,64,1024]{2,1,0:T(8,128)(2,1)S(1)} %get-tuple-element.284), channel_id=1, source_target_pairs={{0,4},{4,8},{8,12},{12,16},{16,20},{20,24},{24,28},{1,5},{5,9},{9,... | collective-permute-start | bytes 786440 | tf_op jit(solution)/shard_map/while/body/eval_jaxpr/ppermute | solution.py:12
  398.9 33.8 %all-gather.2.cloned.1.call-start = ((), (), s32[]{:S(2)}) async-start(), calls=%async_computation | async-start | bytes 1310720 | tf_op jit(solution)/shard_map/while/body/eval_jaxpr/all_gather | solution.py:42
  450.4 3.7 collective-permute-start
  454.1 33.8 %all-gather.2.cloned.1.call-start = ((), (), s32[]{:S(2)}) async-start(), calls=%async_computation | async-start | bytes 1310720 | tf_op jit(solution)/shard_map/while/body/eval_jaxpr/all_gather | solution.py:42
  487.9 10.2 %copy-start.1 = (bf16[2,64,4096]{2,1,0:T(8,128)(2,1)S(1)}, bf16[2,64,4096]{2,1,0:T(8,128)(2,1)}, u32[]{:S(2)}) copy-start(bf16[2,64,4096]{2,1,0:T(8,128)(2,1)} %get-tuple-element.188) | copy-start | bytes 3145732 | tf_op jit(solution)/shard_map/while/body/eval_jaxpr/cond
  505.5 3.7 collective-permute-start
  509.3 33.5 %all-gather.2.cloned.1.call-start = ((), (), s32[]{:S(2)}) async-start(), calls=%async_computation | async-start | bytes 1310720 | tf_op jit(solution)/shard_map/while/body/eval_jaxpr/all_gather | solution.py:42
  560.4 3.7 collective-permute-start
  564.2 33.8 %all-gather.2.cloned.1.call-start = ((), (), s32[]{:S(2)}) async-start(), calls=%async_computation | async-start | bytes 1310720 | tf_op jit(solution)/shard_map/while/body/eval_jaxpr/all_gather | solution.py:42
  615.6 3.7 collective-permute-start
  619.3 33.5 %all-gather.2.cloned.1.call-start = ((), (), s32[]{:S(2)}) async-start(), calls=%async_computation | async-start | bytes 1310720 | tf_op jit(solution)/shard_map/while/body/eval_jaxpr/all_gather | solution.py:42
  670.5 3.7 collective-permute-start
  674.2 33.8 %all-gather.2.cloned.1.call-start = ((), (), s32[]{:S(2)}) async-start(), calls=%async_computation | async-start | bytes 1310720 | tf_op jit(solution)/shard_map/while/body/eval_jaxpr/all_gather | solution.py:42
  725.6 3.8 collective-permute-start
  729.4 33.5 %all-gather.2.cloned.1.call-start = ((), (), s32[]{:S(2)}) async-start(), calls=%async_computation | async-start | bytes 1310720 | tf_op jit(solution)/shard_map/while/body/eval_jaxpr/all_gather | solution.py:42
  780.5 3.7 collective-permute-start
  784.2 33.5 %all-gather.2.cloned.1.call-start = ((), (), s32[]{:S(2)}) async-start(), calls=%async_computation | async-start | bytes 1310720 | tf_op jit(solution)/shard_map/while/body/eval_jaxpr/all_gather | solution.py:42
  817.7 10.2 %copy-start.1 = (bf16[2,64,4096]{2,1,0:T(8,128)(2,1)S(1)}, bf16[2,64,4096]{2,1,0:T(8,128)(2,1)}, u32[]{:S(2)}) copy-start(bf16[2,64,4096]{2,1,0:T(8,128)(2,1)} %get-tuple-element.188) | copy-start | bytes 3145732 | tf_op jit(solution)/shard_map/while/body/eval_jaxpr/cond
  835.3 3.4 collective-permute-start
  (30 other events, 225.0 us)
Sparse Core Ops, SparseCore 0:
  30.0 28.9 all-gather.1
  67.1 39.9 all-gather.1
  115.3 44.3 all-gather.1
  167.5 46.0 all-gather.1
  221.4 46.0 all-gather.1
  275.4 46.9 all-gather.1
  330.5 46.9 all-gather.1
  401.3 31.3 all-gather.1
  456.5 31.3 all-gather.1
  511.4 31.3 all-gather.1
  566.5 31.3 all-gather.1
  621.4 31.3 all-gather.1
  676.6 31.3 all-gather.1
  731.5 31.3 all-gather.1
  786.3 31.3 all-gather.1
where the time goes:
time: 852 us; the launch traced here: 851 us
  waiting for transfers between devices  610 us (72%)
  matrix products  124 us (15%)
  other arithmetic  55.9 us (7%)
  local copies, waits for them, and re-layouts  26.8 us (3%)
  starting transfers between devices  19.2 us (2%)
  between operations  13.1 us (2%)
    all_gather x15, waiting for transfers between devices, beat(): gathered = lax.all_gather(incoming, 'row', axis=2, tiled=True)  558 us
    dot_general x32, matrix products, right_product(): lax.dot_general(left, weights, (((1,), (1,)), ((), ())), preferred_elemen...  124 us
    ppermute x15, waiting for transfers between devices, shifted(): return lax.ppermute(value, axis, pairs)  51.9 us
    select_n x15, other arithmetic, beat(): collected = jnp.where(active, updated, collected)  29.1 us
    select_n x15, other arithmetic, beat(): incoming = jnp.where(level == 0, entering, received)  26.1 us
    ppermute x15, starting transfers between devices, shifted(): return lax.ppermute(value, axis, pairs)  19.2 us
  transfers between devices with their start and end apart: 30, of which 30 were waited for; matrix products, arithmetic and copies ran while one was open for 0% of the time, Pallas kernels for 0%

commit v1 on v0

v1 whole, which is shorter than its diff:
```python
import functools

import jax
import jax.numpy as jnp
from jax import lax
from jax.experimental import pallas as pl
from jax.experimental.pallas import tpu as pltpu
from jax.sharding import PartitionSpec as P

MESH = pl.DeviceIdType.MESH
WIDTH = 32
TILE = 256


def contract(left, weights):
    return lax.dot_general(
        left, weights, (((1,), (1,)), ((), ())), preferred_element_type=jnp.float32
    )


def sweep(
    depth,
    rows,
    operator_ref,
    source_ref,
    entering_ref,
    trace_ref,
    weights,
    incoming,
    outgoing,
    load_sem,
    arrived,
    sent_up,
    sent_down,
    sent_on,
):
    level, me = lax.axis_index("layer"), lax.axis_index("row")
    count, double, local = source_ref.shape
    width = double // 2
    has_up, has_down = me < rows - 1, me > 0
    has_next, has_prev = level < depth - 1, level > 0

    def load(part):
        return pltpu.make_async_copy(
            operator_ref.at[:, 0, :, pl.ds(pl.multiple_of(part * local, local), local)],
            weights.at[part],
            load_sem.at[part],
        )

    def enter(batch):
        return pltpu.make_async_copy(
            entering_ref.at[batch], incoming.at[batch, me], arrived.at[batch, me]
        )

    def along(batch, part, by, sem):
        return pltpu.make_async_remote_copy(
            src_ref=incoming.at[batch, part],
            dst_ref=incoming.at[batch, part],
            send_sem=sem.at[lax.rem(batch, 2), part],
            recv_sem=arrived.at[batch, part],
            device_id={"row": me + by},
            device_id_type=MESH,
        )

    def onward(batch):
        return pltpu.make_async_remote_copy(
            src_ref=outgoing.at[batch],
            dst_ref=incoming.at[batch, me],
            send_sem=sent_on.at[lax.rem(batch, 2)],
            recv_sem=arrived.at[batch, me],
            device_id={"layer": level + 1},
            device_id_type=MESH,
        )

    for part in range(rows):
        load(lax.rem(me + part, rows)).start()

    @pl.when(level == 0)
    def _():
        @pl.loop(0, count)
        def _(batch):
            enter(batch).start()

    barrier = pltpu.get_barrier_semaphore()
    for there, where in (
        (has_up, {"row": me + 1}),
        (has_down, {"row": me - 1}),
        (has_next, {"layer": level + 1}),
        (has_prev, {"layer": level - 1}),
    ):
        @pl.when(there)
        def _(where=where):
            pl.semaphore_signal(barrier, inc=1, device_id=where, device_id_type=MESH)

    pl.semaphore_wait(
        barrier, sum(x.astype(jnp.int32) for x in (has_up, has_down, has_next, has_prev))
    )

    def multiply(batch, part):
        @pl.when(batch == 0)
        def _():
            load(part).wait()

        x = incoming[batch, part]
        for at in range(0, local, TILE):
            cols = slice(at, at + TILE)
            by_re = contract(x, weights[part, 0, cols, :])
            by_im = contract(x, weights[part, 1, cols, :])
            trace_ref[batch, :width, cols] += by_re[:width] - by_im[width:]
            trace_ref[batch, width:, cols] += by_re[width:] + by_im[:width]

    def receive(batch, part):
        pltpu.make_async_copy(
            incoming.at[batch, part], incoming.at[batch, part], arrived.at[batch, part]
        ).wait()

    def drain(batch):
        @pl.loop(0, rows)
        def _(part):
            @pl.when(jnp.logical_and(has_up, part <= me))
            def _():
                along(batch, part, 1, sent_up).wait_send()

            @pl.when(jnp.logical_and(has_down, part >= me))
            def _():
                along(batch, part, -1, sent_down).wait_send()

        @pl.when(has_next)
        def _():
            onward(batch).wait_send()

    @pl.loop(0, count)
    def _(batch):
        trace_ref[batch] = source_ref[batch].astype(jnp.float32)

        @pl.when(batch >= 2)
        def _():
            drain(batch - 2)

        @pl.loop(0, rows)
        def _(hop):
            below, above = me - hop, me + hop
            from_below = below >= 0
            from_above = jnp.logical_and(hop > 0, above < rows)

            @pl.when(from_below)
            def _():
                receive(batch, below)

                @pl.when(has_up)
                def _():
                    along(batch, below, 1, sent_up).start()

            @pl.when(jnp.logical_and(hop == 0, has_down))
            def _():
                along(batch, me, -1, sent_down).start()

            @pl.when(from_above)
            def _():
                receive(batch, above)

                @pl.when(has_down)
                def _():
                    along(batch, above, -1, sent_down).start()

            @pl.when(from_below)
            def _():
                multiply(batch, below)

            @pl.when(from_above)
            def _():
                multiply(batch, above)

        @pl.when(has_next)
        def _():
            outgoing[batch] = trace_ref[batch].astype(jnp.bfloat16)
            onward(batch).start()

    for batch in range(max(count - 2, 0), count):
        drain(batch)


def on_device(depth, rows, operator, sources, boundary):
    local, total = sources.shape[2], sources.shape[3]
    width = WIDTH
    count = total // width

    def batches(value):
        value = jnp.swapaxes(value, 1, 2).reshape(2, count, width, local)
        return jnp.swapaxes(value, 0, 1).reshape(count, 2 * width, local)

    flops = 2 * 4 * local * operator.shape[3] * total
    traces = pl.pallas_call(
        functools.partial(sweep, depth, rows),
        out_shape=jax.ShapeDtypeStruct((count, 2 * width, local), jnp.float32),
        in_specs=[
            pl.BlockSpec(memory_space=pl.ANY),
            pl.BlockSpec(memory_space=pltpu.VMEM),
            pl.BlockSpec(memory_space=pl.ANY),
        ],
        out_specs=pl.BlockSpec(memory_space=pltpu.VMEM),
        scratch_shapes=[
            pltpu.VMEM((rows, 2, local, local), jnp.bfloat16),
            pltpu.VMEM((count, rows, 2 * width, local), jnp.bfloat16),
            pltpu.VMEM((count, 2 * width, local), jnp.bfloat16),
            pltpu.SemaphoreType.DMA((rows,)),
            pltpu.SemaphoreType.DMA((count, rows)),
            pltpu.SemaphoreType.DMA((2, rows)),
            pltpu.SemaphoreType.DMA((2, rows)),
            pltpu.SemaphoreType.DMA((2,)),
        ],
        compiler_params=pltpu.CompilerParams(
            collective_id=0, has_side_effects=True, vmem_limit_bytes=50 << 20
        ),
        cost_estimate=pl.CostEstimate(
            flops=flops, bytes_accessed=2 * operator.size, transcendentals=0
        ),
    )(operator, batches(sources[:, 0]), batches(boundary))
    traces = traces.reshape(count, 2, width, local)
    return traces.transpose(1, 3, 0, 2).reshape(2, 1, local, total)


def solution(mesh):
    placed = (P(None, "layer", "row", None), P(None, "layer", "row", None), P(None, "row", None))
    return jax.shard_map(
        functools.partial(on_device, mesh.shape["layer"], mesh.shape["row"]),
        mesh=mesh,
        in_specs=placed,
        out_specs=P(None, "layer", "row", None),
        check_vma=False,
    )
```

time: 852 us -> 391 us (0.46)
  waiting for transfers between devices: 610 us -> 0 us
  Pallas kernels: 0 us -> 368 us
  matrix products: 124 us -> 0 us
  other arithmetic: 55.9 us -> 0 us
  starting transfers between devices: 19.2 us -> 0 us
  between operations: 13.1 us -> 0.02 us
    all_gather x15 -> x0, waiting for transfers between devices: 558 us -> none  [beat(): gathered = lax.all_gather(incoming, 'row', axis=2, tiled=True)]
    pallas_call x0 -> x1, Pallas kernels: none -> 368 us  [on_device(): pl.pallas_call(functools.partial(sweep, depth, rows), out_shape=jax.Shape...]
    dot_general x32 -> x0, matrix products: 124 us -> none  [right_product(): lax.dot_general(left, weights, (((1,), (1,)), ((), ())), preferred_elemen...]
    select_n x30 -> x0, other arithmetic: 55.2 us -> none  [the longest x15 29.1 us: beat(): collected = jnp.where(active, updated, collected)]
    ppermute x15 -> x0, waiting for transfers between devices: 51.9 us -> none  [shifted(): return lax.ppermute(value, axis, pairs)]
    ppermute x15 -> x0, starting transfers between devices: 19.2 us -> none  [shifted(): return lax.ppermute(value, axis, pairs)]
    squeeze x1 -> x0, local copies, waits for them, and re-layouts: 11.7 us -> none  [on_device(): imag = operator[1, 0]]
    reshape x0 -> x2, local copies, waits for them, and re-layouts: none -> 10.1 us  [the longest x1 5.36 us: on_device(): return traces.transpose(1, 3, 0, 2).reshape(2, 1, local, total)]
  transfers between devices with their start and end apart: 30 -> 0, of which waited for: 30 -> 0; matrix products, arithmetic and copies ran while one was open for 0% -> 0% of each run, Pallas kernels for 0% -> 0%
where the time goes in v1:
time: 391 us
  Pallas kernels  368 us (94%)
  local copies, waits for them, and re-layouts  22.9 us (6%)
    pallas_call x1, Pallas kernels, on_device(): pl.pallas_call(functools.partial(sweep, depth, rows), out_shape=jax.Shape...  368 us
    unnamed x2, local copies, waits for them, and re-layouts  7.84 us

profile of v1, /device:TPU:7, one launch (start us, length us, event | category | flops | bytes accessed | tf_op | source)
XLA Modules:
  0.0 390.9 jit_solution(4478624115758871690)
XLA Ops:
  0.0 3.9 %copy.7 = bf16[2,1,1024,512]{2,3,0,1:T(8,128)(2,1)} copy(bf16[2,1,1024,512]{3,2,1,0:T(8,128)(2,1)} %param.4) | data formatting | bytes 4194304 | tf_op args[1]
  3.9 1.8 copy.8
  5.7 3.9 %copy.9 = bf16[2,1024,512]{1,2,0:T(8,128)(2,1)} copy(bf16[2,1024,512]{2,1,0:T(8,128)(2,1)} %param.5) | data formatting | bytes 4194304 | tf_op args[2]
  9.7 3.2 copy.10
  12.8 367.9 %shard_map.37 = f32[16,64,1024]{2,1,0:T(8,128)} custom-call(bf16[2,1,1024,4096]{3,2,1,0:T(8,128)(2,1)} %operator_ref.1, bf16[16,64,1024]{2,1,0:T(8,128)(2,1)S(1)} %bitcast.18, bf16[16,64,1024]{2,1,0:T(8,128)(2,1)} %bitcast.23), custom_call_target="tpu_custom_call" | custom-call | flops 17179869184 | bytes 16777216 | tf_op jit(solution)/shard_map/pallas_call | solution.py:193
  380.8 4.7 %copy.11 = f32[16,2,32,1024]{3,2,0,1:T(8,128)} copy(f32[16,2,32,1024]{3,2,1,0:T(8,128)} %bitcast.22) | data formatting | bytes 8388608 | tf_op jit(solution)/shard_map/reshape | solution.py:219
  385.5 5.4 %copy.12 = f32[2,1,1024,512]{3,2,1,0:T(8,128)} copy(f32[2,1,1024,512]{2,3,0,1:T(8,128)} %bitcast.19) | data formatting | bytes 8388608 | tf_op jit(solution)/shard_map/reshape | solution.py:220

commit v2 on v1

v2 whole, which is shorter than its diff:
```python
import functools

import jax
import jax.numpy as jnp
from jax import lax
from jax.experimental import pallas as pl
from jax.experimental.pallas import tpu as pltpu
from jax.sharding import PartitionSpec as P

MESH = pl.DeviceIdType.MESH
WIDTH = 32
TILE = 256
REACH = 2
NEAR = (2, -2, 1, -1)
SLOTS = 4


def contract(left, weights):
    return lax.dot_general(
        left, weights, (((1,), (1,)), ((), ())), preferred_element_type=jnp.float32
    )


def sweep(
    depth,
    rows,
    operator_ref,
    source_ref,
    entering_ref,
    trace_ref,
    weights,
    incoming,
    outgoing,
    load_sem,
    arrived,
    sent_first,
    sent_on,
    passed,
):
    level, me = lax.axis_index("layer"), lax.axis_index("row")
    count, _, _, width, local = incoming.shape
    has_next, has_prev = level < depth - 1, level > 0
    first, last = level == 0, level == depth - 1
    others = [side * by for by in range(1, rows) for side in (1, -1)]

    def inside(row):
        return jnp.logical_and(row >= 0, row < rows)

    def both(*flags):
        return functools.reduce(jnp.logical_and, flags)

    def columns(batch):
        return pl.ds(pl.multiple_of(batch * width, width), width)

    def load(part):
        return pltpu.make_async_copy(
            operator_ref.at[:, 0, :, pl.ds(pl.multiple_of(part * local, local), local)],
            weights.at[part],
            load_sem.at[part],
        )

    def enter(batch):
        return pltpu.make_async_copy(
            entering_ref.at[:, columns(batch)], incoming.at[batch, me], arrived.at[batch, me]
        )

    def send_first(batch, by):
        return pltpu.make_async_remote_copy(
            src_ref=entering_ref.at[:, columns(batch)],
            dst_ref=incoming.at[batch, me],
            send_sem=sent_first.at[lax.rem(batch, SLOTS), by + rows - 1],
            recv_sem=arrived.at[batch, me],
            device_id={"layer": lax.rem(level + 1, depth), "row": me + by},
            device_id_type=MESH,
        )

    def send_on(batch, by):
        return pltpu.make_async_remote_copy(
            src_ref=outgoing.at[batch],
            dst_ref=incoming.at[batch, me],
            send_sem=sent_on.at[lax.rem(batch, 2), by + REACH],
            recv_sem=arrived.at[batch, me],
            device_id={"layer": level + 1, "row": me + by},
            device_id_type=MESH,
        )

    def forward(batch, part, by):
        return pltpu.make_async_remote_copy(
            src_ref=incoming.at[batch, part],
            dst_ref=incoming.at[batch, part],
            send_sem=passed.at[lax.rem(batch, 2), part],
            recv_sem=arrived.at[batch, part],
            device_id={"row": me + by},
            device_id_type=MESH,
        )

    @pl.when(first)
    def _():
        @pl.loop(0, count)
        def _(batch):
            enter(batch).start()

    for part in range(rows):
        load(lax.rem(me + part, rows)).start()

    barrier = pltpu.get_barrier_semaphore()
    peers = [(inside(me + by), {"row": me + by}) for by in (1, -1)]
    for by in others:
        peers.append((both(first, inside(me + by)), {"layer": lax.rem(level + depth - 1, depth), "row": me + by}))
        peers.append((both(last, inside(me + by)), {"layer": lax.rem(level + 1, depth), "row": me + by}))
    for by in (*NEAR, 0):
        peers.append((both(has_next, inside(me + by)), {"layer": level + 1, "row": me + by}))
        peers.append((both(has_prev, inside(me + by)), {"layer": level - 1, "row": me + by}))
    for there, where in peers:
        @pl.when(there)
        def _(where=where):
            pl.semaphore_signal(barrier, inc=1, device_id=where, device_id_type=MESH)
    pl.semaphore_wait(barrier, sum(there.astype(jnp.int32) for there, _ in peers))

    def settle(batch):
        for by in others:
            @pl.when(inside(me + by))
            def _(by=by):
                send_first(batch, by).wait_send()

    @pl.when(last)
    def _():
        @pl.loop(0, count)
        def _(batch):
            @pl.when(batch >= SLOTS)
            def _():
                settle(batch - SLOTS)

            for by in others:
                @pl.when(inside(me + by))
                def _(by=by):
                    send_first(batch, by).start()

        @pl.loop(max(count - SLOTS, 0), count)
        def _(batch):
            settle(batch)

    def multiply(batch, part):
        @pl.when(batch == 0)
        def _():
            load(part).wait()

        x = incoming[batch, part].reshape(2 * width, local)
        for at in range(0, local, TILE):
            cols = slice(at, at + TILE)
            by_re = contract(x, weights[part, 0, cols, :])
            by_im = contract(x, weights[part, 1, cols, :])
            trace_ref[0, columns(batch), cols] += by_re[:width] - by_im[width:]
            trace_ref[1, columns(batch), cols] += by_re[width:] + by_im[:width]

    def receive(batch, part):
        pltpu.make_async_copy(
            incoming.at[batch, part], incoming.at[batch, part], arrived.at[batch, part]
        ).wait()

    def drain(batch):
        for by in (*NEAR, 0):
            @pl.when(both(has_next, inside(me + by)))
            def _(by=by):
                send_on(batch, by).wait_send()

        @pl.loop(0, rows)
        def _(part):
            @pl.when(both(has_prev, me - part >= REACH, me < rows - 1))
            def _():
                forward(batch, part, 1).wait_send()

            @pl.when(both(has_prev, part - me >= REACH, me > 0))
            def _():
                forward(batch, part, -1).wait_send()

    def take(batch, distance, side):
        part = me - side * distance
        @pl.when(inside(part))
        def _():
            receive(batch, part)

            @pl.when(both(has_prev, distance >= REACH, inside(me + side)))
            def _():
                forward(batch, part, side).start()

    @pl.loop(0, count)
    def _(batch):
        trace_ref[:, columns(batch)] = source_ref[:, columns(batch)].astype(jnp.float32)

        @pl.when(batch >= 2)
        def _():
            drain(batch - 2)

        @pl.loop(0, rows)
        def _(distance):
            @pl.when(distance == 1)
            def _():
                take(batch, REACH, 1)
                take(batch, REACH, -1)

            for side in (1, -1):
                part = me - side * distance

                @pl.when(jnp.logical_and(distance != REACH, distance > 0 if side < 0 else distance >= 0))
                def _(side=side):
                    take(batch, distance, side)

                @pl.when(jnp.logical_and(inside(part), distance > 0 if side < 0 else distance >= 0))
                def _(part=part):
                    multiply(batch, part)

        @pl.when(has_next)
        def _():
            outgoing[batch] = trace_ref[:, columns(batch)].astype(jnp.bfloat16)
            for by in (*NEAR, 0):
                @pl.when(inside(me + by))
                def _(by=by):
                    send_on(batch, by).start()

    for batch in range(max(count - 2, 0), count):
        drain(batch)


def on_device(depth, rows, operator, sources, boundary):
    local, total = sources.shape[2], sources.shape[3]
    width = WIDTH
    count = total // width

    flops = 2 * 4 * local * operator.shape[3] * total
    traces = pl.pallas_call(
        functools.partial(sweep, depth, rows),
        out_shape=jax.ShapeDtypeStruct((2, total, local), jnp.float32),
        in_specs=[
            pl.BlockSpec(memory_space=pl.ANY),
            pl.BlockSpec(memory_space=pltpu.VMEM),
            pl.BlockSpec(memory_space=pl.ANY),
        ],
        out_specs=pl.BlockSpec(memory_space=pltpu.VMEM),
        scratch_shapes=[
            pltpu.VMEM((rows, 2, local, local), jnp.bfloat16),
            pltpu.VMEM((count, rows, 2, width, local), jnp.bfloat16),
            pltpu.VMEM((count, 2, width, local), jnp.bfloat16),
            pltpu.SemaphoreType.DMA((rows,)),
            pltpu.SemaphoreType.DMA((count, rows)),
            pltpu.SemaphoreType.DMA((SLOTS, 2 * rows - 1)),
            pltpu.SemaphoreType.DMA((2, 2 * REACH + 1)),
            pltpu.SemaphoreType.DMA((2, rows)),
        ],
        compiler_params=pltpu.CompilerParams(
            collective_id=0, has_side_effects=True, vmem_limit_bytes=50 << 20
        ),
        cost_estimate=pl.CostEstimate(
            flops=flops, bytes_accessed=2 * operator.size, transcendentals=0
        ),
    )(operator, jnp.swapaxes(sources[:, 0], 1, 2), jnp.swapaxes(boundary, 1, 2))
    return jnp.swapaxes(traces, 1, 2)[:, None]


def solution(mesh):
    placed = (P(None, "layer", "row", None), P(None, "layer", "row", None), P(None, "row", None))
    return jax.shard_map(
        functools.partial(on_device, mesh.shape["layer"], mesh.shape["row"]),
        mesh=mesh,
        in_specs=placed,
        out_specs=P(None, "layer", "row", None),
        check_vma=False,
    )
```

time: 391 us -> 261 us (0.67)
  Pallas kernels: 368 us -> 249 us
  local copies, waits for them, and re-layouts: 22.9 us -> 12.3 us
    pallas_call x1, Pallas kernels: 368 us -> 249 us  [on_device(): pl.pallas_call(functools.partial(sweep, depth, rows), out_shape=jax.Shape...]
    reshape x2 -> x0, local copies, waits for them, and re-layouts: 10.1 us -> none  [the longest x1 5.36 us: on_device(): return traces.transpose(1, 3, 0, 2).reshape(2, 1, local, total)]
    broadcast_in_dim x0 -> x1, local copies, waits for them, and re-layouts: none -> 5.37 us  [on_device(): return jnp.swapaxes(traces, 1, 2)[:, None]]
    transpose x2 -> x0, local copies, waits for them, and re-layouts: 5 us -> none  [batches(): return jnp.swapaxes(value, 0, 1).reshape(count, 2 * width, local)]
where the time goes in v2:
time: 261 us
  Pallas kernels  249 us (95%)
  local copies, waits for them, and re-layouts  12.3 us (5%)
    pallas_call x1, Pallas kernels, on_device(): pl.pallas_call(functools.partial(sweep, depth, rows), out_shape=jax.Shape...  249 us
    unnamed x2, local copies, waits for them, and re-layouts  6.91 us
    broadcast_in_dim x1, local copies, waits for them, and re-layouts, on_device(): return jnp.swapaxes(traces, 1, 2)[:, None]  5.37 us

profile of v2, /device:TPU:7, one launch (start us, length us, event | category | flops | bytes accessed | tf_op | source)
XLA Modules:
  0.0 261.2 jit_solution(12104615888004106145)
XLA Ops:
  0.0 3.0 %copy.4 = bf16[2,1,1024,512]{2,3,0,1:T(8,128)(2,1)S(1)} copy(bf16[2,1,1024,512]{3,2,1,0:T(8,128)(2,1)} %param.4) | data formatting | bytes 4194304 | tf_op args[1]
  3.0 3.9 %copy.5 = bf16[2,1024,512]{1,2,0:T(8,128)(2,1)} copy(bf16[2,1024,512]{2,1,0:T(8,128)(2,1)} %param.5) | data formatting | bytes 4194304 | tf_op args[2]
  6.9 248.9 %shard_map.37 = f32[2,512,1024]{2,1,0:T(8,128)} custom-call(bf16[2,1,1024,4096]{3,2,1,0:T(8,128)(2,1)} %operator_ref.1, bf16[2,512,1024]{2,1,0:T(8,128)(2,1)S(1)} %bitcast.7, bf16[2,512,1024]{2,1,0:T(8,128)(2,1)} %bitcast.9), custom_call_target="tpu_custom_call" | custom-call | flops 17179869184 | bytes 16777216 | tf_op jit(solution)/shard_map/pallas_call | solution.py:231
  255.8 5.4 %copy.6 = f32[2,1,1024,512]{3,2,1,0:T(8,128)} copy(f32[2,1,1024,512]{2,3,0,1:T(8,128)} %bitcast.8) | data formatting | bytes 8388608 | tf_op jit(solution)/shard_map/broadcast_in_dim | solution.py:257
